TPU v7x, 32 devices: a whole 2x2x4 slice. The times are simulated.
32 devices in a mesh: groups: 2 (over x), ctx: 16 (over z, y, core).
Axes of the slice: x: 2, y: 2, z: 4, core: 2. Of those that a mesh axis runs over, the one named last changes fastest.
Arguments:
- queries: bfloat16 [256, 8192], P(('groups', 'ctx')), parts along dimension 0, may hold values from -8 to 8
- prefix_key_heads: bfloat16 [16384, 1024], P(('groups', 'ctx')), parts along dimension 0, may hold values from -8 to 8
- prefix_value_heads: bfloat16 [16384, 1024], P(('groups', 'ctx')), parts along dimension 0, may hold values from -6 to 6
- tree_key_heads: bfloat16 [256, 1024], P(('groups', 'ctx')), parts along dimension 0, may hold values from -16 to 16
- tree_value_heads: bfloat16 [256, 1024], P(('groups', 'ctx')), parts along dimension 0, may hold values from -6 to 6
- token_embed: bfloat16 [256, 8192], P(('groups', 'ctx')), parts along dimension 0, may hold values from -12 to 12
- fc_embed: bfloat16 [8192, 8192], P('ctx'), may hold values from -0.25 to 0.25
- fc_feature: bfloat16 [8192, 8192], P('ctx'), may hold values from -0.0625 to 0.0625
- draft_gain: float32 [8192], replicated, may hold values from 0.5 to 1.5
- parents: int32 [4, 64], P('groups'), parts along dimension 0, may hold values from 0 to 62, as said below
- accepted: int32 [4], P('groups'), parts along dimension 0, may hold values from 0 to 63, as said below
Outputs:
- attended: bfloat16 [256, 8192], P(('groups', 'ctx')), parts along dimension 0
- draft_input: bfloat16 [256, 8192], P(('groups', 'ctx')), parts along dimension 0
There are 2 independent parts, one for each index of `groups`. A program takes and returns all parts, laid end to end along the dimension named above; an argument that names none is the same for every part. Nothing has to cross between parts.
Inputs may be any that keep to these rules, and one draw needn't show every extreme that they name: parents[t, 0] = 0 marks the root; every other node's parent is an earlier node of the same tree; no node lies more than 6 steps below its root, and every tree has a node exactly 6 steps below it. The accepted rows of tree t are node accepted[t] and all its ancestors, so at most 7 rows a tree; in every draw some tree accepts exactly 7 rows.
All inputs are finite; a program needn't handle non-finite values.
Results may differ from a plain program's by a relative error of at most 0.0028.
Values may be sent and summed in bfloat16 or wider, within the bound.
A program may use at most 128 MiB of HBM per device.

v0:
```python
import jax
import jax.numpy as jnp
from jax import lax
from jax.sharding import PartitionSpec as P

QUERY_HEADS = 64
KEY_HEADS = 8
HEAD_WIDTH = 128


highest = lax.Precision.HIGHEST
negative_fill = -1e30


def ancestors(parents):
    nodes = parents.shape[1]
    column = jnp.arange(nodes, dtype=jnp.int32)
    upward = (parents[:, :, None] == column[None, None, :]).astype(jnp.float32)
    closure = jnp.maximum(upward, jnp.eye(nodes, dtype=jnp.float32)[None])
    for repeat in range(max(1, (nodes - 1).bit_length())):
        closure = jnp.minimum(jnp.einsum("tij,tjk->tik", closure, closure, precision=highest), 1.0)
    return closure


def prefix_partial(gathered_q, keys_local, values_local):
    every_row = gathered_q.shape[0]
    queries_per_group = QUERY_HEADS // KEY_HEADS
    scale_factor = HEAD_WIDTH ** (-0.5)
    numerators = []
    denominators = []
    maxima = []
    for key_value_group in range(KEY_HEADS):
        group_q = gathered_q[
            :,
            key_value_group
            * queries_per_group
            * HEAD_WIDTH : (key_value_group + 1)
            * queries_per_group
            * HEAD_WIDTH,
        ].reshape(every_row * queries_per_group, HEAD_WIDTH)
        group_k = keys_local[:, key_value_group * HEAD_WIDTH : (key_value_group + 1) * HEAD_WIDTH]
        group_v = values_local[:, key_value_group * HEAD_WIDTH : (key_value_group + 1) * HEAD_WIDTH]
        scores = (
            jnp.einsum("qd,kd->qk", group_q, group_k, preferred_element_type=jnp.float32)
            * scale_factor
        )
        block_max = jnp.max(scores, axis=1)
        weights = jnp.exp(scores - block_max[:, None])
        denominators.append(jnp.sum(weights, axis=1).reshape(every_row, queries_per_group))
        maxima.append(block_max.reshape(every_row, queries_per_group))
        block_num = jnp.dot(
            weights.astype(jnp.bfloat16), group_v, preferred_element_type=jnp.float32
        )
        numerators.append(block_num.reshape(every_row, queries_per_group * HEAD_WIDTH))
    return (
        jnp.concatenate(numerators, axis=1),
        jnp.concatenate(denominators, axis=1),
        jnp.concatenate(maxima, axis=1),
    )


def tree_part(own_query, every_key, every_value, allowed):
    owned_rows = own_query.shape[0]
    every_row = every_key.shape[0]
    queries_per_group = QUERY_HEADS // KEY_HEADS
    split_query = own_query.reshape(owned_rows, KEY_HEADS, queries_per_group, HEAD_WIDTH)
    split_key = every_key.reshape(every_row, KEY_HEADS, HEAD_WIDTH)
    split_value = every_value.reshape(every_row, KEY_HEADS, HEAD_WIDTH)
    scores = jnp.einsum(
        "rgid,jgd->rgij", split_query, split_key, preferred_element_type=jnp.float32
    ) * HEAD_WIDTH ** (-0.5)
    scores = jnp.where(allowed[:, None, None, :] > 0.5, scores, negative_fill)
    tree_maximum = jnp.max(scores, axis=3)
    weights = jnp.exp(scores - tree_maximum[..., None])
    tree_denominator = jnp.sum(weights, axis=3)
    tree_numerator = jnp.einsum(
        "rgij,jgd->rgid",
        weights.astype(jnp.bfloat16),
        split_value,
        preferred_element_type=jnp.float32,
    )
    return (
        tree_numerator.reshape(owned_rows, QUERY_HEADS * HEAD_WIDTH),
        tree_denominator.reshape(owned_rows, QUERY_HEADS),
        tree_maximum.reshape(owned_rows, QUERY_HEADS),
    )


def finish(pref_num, pref_den, pref_max, tree_numerator, tree_denominator, tree_maximum):
    owned_rows = pref_num.shape[0]
    final_max = jnp.maximum(pref_max, tree_maximum)
    pref_scale = jnp.exp(pref_max - final_max)
    tree_scale = jnp.exp(tree_maximum - final_max)
    numer = (
        pref_num.reshape(owned_rows, QUERY_HEADS, HEAD_WIDTH) * pref_scale[..., None]
        + tree_numerator.reshape(owned_rows, QUERY_HEADS, HEAD_WIDTH) * tree_scale[..., None]
    )
    denom = pref_den * pref_scale + tree_denominator * tree_scale
    return (
        (numer / denom[..., None])
        .reshape(owned_rows, QUERY_HEADS * HEAD_WIDTH)
        .astype(jnp.bfloat16)
    )


def body(
    queries,
    prefix_key_heads,
    prefix_value_heads,
    tree_key_heads,
    tree_value_heads,
    token_embed,
    fc_embed,
    fc_feature,
    draft_gain,
    parents,
    accepted,
):
    tree_count = parents.shape[0]
    node_count = parents.shape[1]
    owned_rows = queries.shape[0]
    every_row = tree_count * node_count
    ctx_size = lax.axis_size("ctx")
    first_row = lax.axis_index("ctx") * owned_rows
    closure = ancestors(parents)
    chosen = (accepted[:, None] == jnp.arange(node_count, dtype=jnp.int32)[None, :]).astype(
        jnp.float32
    )
    on_path = jnp.einsum("ti,tij->tj", chosen, closure, precision=highest)
    own_reach = lax.dynamic_slice_in_dim(
        closure.reshape(every_row, node_count), first_row, owned_rows, 0
    )
    own_rows = first_row + jnp.arange(owned_rows, dtype=jnp.int32)
    own_tree = own_rows // node_count
    same_tree = (jnp.arange(tree_count, dtype=jnp.int32)[None, :] == own_tree[:, None]).astype(
        jnp.float32
    )
    allowed = (same_tree[:, :, None] * own_reach[:, None, :]).reshape(owned_rows, every_row)
    own_path = lax.dynamic_slice_in_dim(on_path.reshape(every_row), first_row, owned_rows, 0)
    gathered_q, gathered_k, gathered_v = (
        lax.all_gather(queries, "ctx", axis=0, tiled=True),
        lax.all_gather(tree_key_heads, "ctx", axis=0, tiled=True),
        lax.all_gather(tree_value_heads, "ctx", axis=0, tiled=True),
    )
    pref_num, pref_den, pref_max = prefix_partial(gathered_q, prefix_key_heads, prefix_value_heads)
    piece_num, piece_den, piece_max = (
        lax.all_to_all(pref_num[None], "ctx", split_axis=1, concat_axis=0, tiled=True),
        lax.all_to_all(pref_den[None], "ctx", split_axis=1, concat_axis=0, tiled=True),
        lax.all_to_all(pref_max[None], "ctx", split_axis=1, concat_axis=0, tiled=True),
    )
    own_max = jnp.max(piece_max, axis=0)
    factor = jnp.exp(piece_max - own_max[None])
    own_num = jnp.sum(
        piece_num.reshape(ctx_size, owned_rows, QUERY_HEADS, HEAD_WIDTH) * factor[..., None], axis=0
    ).reshape(owned_rows, QUERY_HEADS * HEAD_WIDTH)
    own_den = jnp.sum(piece_den * factor, axis=0)
    tree_numerator, tree_denominator, tree_maximum = tree_part(
        queries, gathered_k, gathered_v, allowed
    )
    attended = finish(own_num, own_den, own_max, tree_numerator, tree_denominator, tree_maximum)
    embed_cols, feature_cols = (
        lax.all_to_all(token_embed, "ctx", split_axis=1, concat_axis=0, tiled=True),
        lax.all_to_all(attended, "ctx", split_axis=1, concat_axis=0, tiled=True),
    )
    own_joined = lax.psum_scatter(
        jnp.dot(embed_cols, fc_embed, preferred_element_type=jnp.float32)
        + jnp.dot(feature_cols, fc_feature, preferred_element_type=jnp.float32),
        "ctx",
        scatter_dimension=0,
        tiled=True,
    )
    mean_square = jnp.mean(own_joined * own_joined, axis=1, keepdims=True)
    normed = own_joined * lax.rsqrt(mean_square + 1e-06) * draft_gain[None, :]
    draft_input = jnp.where(own_path[:, None] > 0.5, normed, 0.0).astype(jnp.bfloat16)
    return (attended, draft_input)


def solution(mesh):
    placed = (
        P(("groups", "ctx"), None),
        P(("groups", "ctx"), None),
        P(("groups", "ctx"), None),
        P(("groups", "ctx"), None),
        P(("groups", "ctx"), None),
        P(("groups", "ctx"), None),
        P("ctx", None),
        P("ctx", None),
        P(),
        P("groups", None),
        P("groups"),
    )
    return jax.shard_map(
        body,
        mesh=mesh,
        in_specs=placed,
        out_specs=(P(("groups", "ctx"), None), P(("groups", "ctx"), None)),
        check_vma=False,
    )
```

profile of v0, /device:TPU:0, one launch (start us, length us, event | category | flops | bytes accessed | tf_op | source)
XLA Modules:
  0.0 386.1 jit_solution(749761643524574976)
XLA Ops:
  7.9 46.4 %all-gather.2.cloned.1.call-done = bf16[128,8192]{1,0:T(8,128)(2,1)} async-done(((bf16[8,8192]{1,0:T(8,128)(2,1)}), bf16[128,8192]{1,0:T(8,128)(2,1)}) %all-gather.2.cloned.1.call-update) | async-done | bytes 2097168 | tf_op jit(solution)/shard_map/all_gather | solution.py:141
  54.3 2.5 fusion.108
  57.8 1.3 multiply_reduce_fusion.8
  59.6 1.4 fusion.32
  61.0 1.4 multiply_reduce_fusion.7
  62.8 1.5 fusion.30
  64.5 1.3 multiply_reduce_fusion.6
  66.2 1.5 fusion.28
  68.5 1.3 multiply_reduce_fusion.5
  70.3 1.5 fusion.26
  72.6 1.3 multiply_reduce_fusion.4
  73.9 1.0 fusion.8
  74.9 2.2 fusion.24
  77.9 1.3 multiply_reduce_fusion.3
  79.3 1.0 fusion.10
  80.2 2.2 fusion.22
  82.7 1.3 multiply_reduce_fusion.2
  84.0 1.0 fusion.12
  85.0 2.2 fusion.20
  88.1 1.3 multiply_reduce_fusion.1
  89.4 1.0 fusion.14
  90.4 2.2 fusion.18
  93.4 0.9 reshape.308
  94.7 1.1 reshape.314
  95.9 1.1 reshape.318
  97.1 1.7 concatenate.10
  99.3 1.6 reduce.3
  101.6 3.5 all-to-all-start.1
  105.1 0.8 constant_dynamic-update-slice_fusion.7
  105.9 1.9 constant_dynamic-update-slice_fusion.6
  110.3 0.8 constant_dynamic-update-slice_fusion.2
  111.2 0.9 constant_dynamic-update-slice_fusion.1
  114.5 6.0 %all-to-all-start.2 = ((f32[16,1,512]{2,1,0:T(1,128)}), f32[16,1,512]{2,1,0:T(1,128)S(1)}, u32[]{:S(2)}, u32[]{:S(2)}) async-start(f32[16,1,512]{2,1,0:T(1,128)} %reshape.350), calls=%async_computation.2 | async-start | bytes 65536 | tf_op jit(solution)/shard_map/all_to_all | solution.py:148
  121.4 6.6 %broadcast_in_dim.22 = f32[1,128,8192]{2,0,1:T(1,128)} reshape(f32[128,8192]{1,0:T(8,128)} %constant_dynamic-update-slice_fusion) | data formatting | bytes 8388608 | tf_op jit(solution)/shard_map/broadcast_in_dim | solution.py:147
  128.0 6.2 %all-to-all-start = ((f32[1,128,8192]{2,0,1:T(1,128)}), f32[1,128,8192]{2,0,1:T(1,128)}, u32[]{:S(2)}, u32[]{:S(2)}) async-start(f32[1,128,8192]{2,0,1:T(1,128)} %broadcast_in_dim.22), calls=%async_computation | async-start | bytes 8388608 | tf_op jit(solution)/shard_map/all_to_all | solution.py:147
  135.8 86.5 %all_gather.10 = bf16[128,1024]{1,0:T(8,128)(2,1)S(1)} all-gather(bf16[8,1024]{1,0:T(8,128)(2,1)S(1)} %copy-done.15), channel_id=1, replica_groups=mesh['groups'=2,'ctx'=16] {'ctx'}, dimensions={0}, use_global_device_ids=true | all-gather | bytes 278528 | tf_op jit(solution)/shard_map/all_gather | solution.py:142
  223.2 35.8 %all_gather.11 = bf16[128,1024]{1,0:T(8,128)(2,1)S(1)} all-gather(bf16[8,1024]{1,0:T(8,128)(2,1)S(1)} %copy-done.16), channel_id=1, replica_groups=mesh['groups'=2,'ctx'=16] {'ctx'}, dimensions={0}, use_global_device_ids=true | all-gather | bytes 278528 | tf_op jit(solution)/shard_map/all_gather | solution.py:143
  261.7 3.5 all-to-all-start.3
  265.2 2.6 mul.154
  267.8 13.1 %multiply_reduce_fusion = f32[8,8192]{1,0:T(8,128)S(1)} fusion(f32[1,16,8,8192]{3,0,2,1:T(1,128)} %bitcast, f32[1,16,8,8192]{3,0,2,1:T(1,128)} %bitcast.92), kind=kLoop, calls=%fused_computation.1 | loop fusion | flops 2031616 | bytes 8650752 | tf_op jit(solution)/shard_map/reduce_sum | solution.py:153
  282.0 6.0 %all-to-all-start.4 = ((bf16[8,16,512]{2,0,1:T(8,128)(2,1)}), bf16[8,16,512]{2,0,1:T(8,128)(2,1)S(1)}, u32[]{:S(2)}, u32[]{:S(2)}) async-start(bf16[8,16,512]{2,0,1:T(8,128)(2,1)} %copy.83), calls=%async_computation.4 | async-start | bytes 262144 | tf_op jit(solution)/shard_map/all_to_all | solution.py:163
  288.2 6.6 %fusion.60 = f32[128,8192]{1,0:T(8,128)} fusion(bf16[512,8192]{1,0:T(8,128)(2,1)} %param.17, bf16[8,16,512]{2,0,1:T(8,128)(2,1)S(1)} %all-to-all-done.3), kind=kOutput, calls=%fused_computation.83 | convolution fusion | flops 1073741824 | bytes 12713984 | tf_op jit(solution)/shard_map/dot_general | solution.py:166
  294.8 1.1 all-to-all-done.4
  295.9 7.8 %convolution_add_fusion = f32[128,8192]{1,0:T(8,128)} fusion(f32[128,8192]{1,0:T(8,128)} %fusion.60, bf16[512,8192]{1,0:T(8,128)(2,1)} %param.18, bf16[8,16,512]{2,0,1:T(8,128)(2,1)S(1)} %all-to-all-done.4), kind=kOutput, calls=%fused_computation | convolution fusion | flops 1074790400 | bytes 16908288 | tf_op jit(solution)/shard_map/dot_general | solution.py:167
  305.0 0.9 fusion.52
  305.9 70.5 %reduce-scatter.2.cloned.1.call-done = f32[8,8192]{1,0:T(8,128)} async-done(((f32[128,8192]{1,0:T(8,128)}), f32[8,8192]{1,0:T(8,128)}) %reduce-scatter.2.cloned.1.call-update) | async-done | bytes 262160 | tf_op jit(solution)/shard_map/reduce_scatter | solution.py:165
  376.4 1.1 multiply_reduce_fusion.9
  377.6 1.7 select_convert_fusion
  (134 shorter events, 22.6 us)
Async XLA Ops:
  7.2 47.1 %all-gather.2.cloned.1.call-start = ((), (), s32[]{:S(2)}) async-start(), calls=%async_computation.6 | async-start | bytes 2228224 | tf_op jit(solution)/shard_map/all_gather | solution.py:141
  59.2 1.8 copy-start.5
  62.8 1.6 copy-start.4
  66.2 2.2 copy-start.3
  70.3 2.2 copy-start.2
  94.3 1.5 copy-start.1
  94.4 2.7 copy-start.6
  94.4 2.7 copy-start.7
  94.4 2.7 copy-start.8
  101.6 12.9 %all-to-all-start.1 = ((f32[16,1,512]{2,1,0:T(1,128)}), f32[16,1,512]{2,1,0:T(1,128)S(1)}, u32[]{:S(2)}, u32[]{:S(2)}) async-start(f32[16,1,512]{2,1,0:T(1,128)} %reshape.348), calls=%async_computation.1 | async-start | bytes 65536 | tf_op jit(solution)/shard_map/all_to_all | solution.py:149
  108.7 3.7 copy-start.11
  108.7 3.8 copy-start.12
  108.7 3.9 %copy-start.13 = (f32[1024]{0:T(1024)S(1)}, f32[1024]{0:T(1024)}, u32[]{:S(2)}) copy-start(f32[1024]{0:T(1024)} %fusion.12) | copy-start | bytes 12292
  108.7 4.0 %copy-start = (f32[1024,128]{1,0:T(8,128)S(1)}, f32[1024,128]{1,0:T(8,128)}, u32[]{:S(2)}) copy-start(f32[1024,128]{1,0:T(8,128)} %fusion.18) | copy-start | bytes 1572868
  109.5 3.3 copy-start.14
  114.5 13.4 %all-to-all-start.2 = ((f32[16,1,512]{2,1,0:T(1,128)}), f32[16,1,512]{2,1,0:T(1,128)S(1)}, u32[]{:S(2)}, u32[]{:S(2)}) async-start(f32[16,1,512]{2,1,0:T(1,128)} %reshape.350), calls=%async_computation.2 | async-start | bytes 65536 | tf_op jit(solution)/shard_map/all_to_all | solution.py:148
  128.0 6.3 %copy-start.17 = (s32[2,64]{1,0:T(2,128)S(1)}, s32[2,64]{1,0:T(2,128)}, u32[]{:S(2)}) copy-start(s32[2,64]{1,0:T(2,128)} %param.20) | copy-start | bytes 1540
  128.0 7.8 %copy-start.15 = (bf16[8,1024]{1,0:T(8,128)(2,1)S(1)}, bf16[8,1024]{1,0:T(8,128)(2,1)}, u32[]{:S(2)}) copy-start(bf16[8,1024]{1,0:T(8,128)(2,1)} %param.14) | copy-start | bytes 49156
  128.0 94.5 %copy-start.9 = (bf16[8,8192]{1,0:T(8,128)(2,1)S(1)}, bf16[8,8192]{1,0:T(8,128)(2,1)}, u32[]{:S(2)}) copy-start(bf16[8,8192]{1,0:T(8,128)(2,1)} %param.11) | copy-start | bytes 393220
  128.0 133.7 %all-to-all-start = ((f32[1,128,8192]{2,0,1:T(1,128)}), f32[1,128,8192]{2,0,1:T(1,128)}, u32[]{:S(2)}, u32[]{:S(2)}) async-start(f32[1,128,8192]{2,0,1:T(1,128)} %broadcast_in_dim.22), calls=%async_computation | async-start | bytes 8388608 | tf_op jit(solution)/shard_map/all_to_all | solution.py:147
  134.2 89.0 %copy-start.16 = (bf16[8,1024]{1,0:T(8,128)(2,1)S(1)}, bf16[8,1024]{1,0:T(8,128)(2,1)}, u32[]{:S(2)}) copy-start(bf16[8,1024]{1,0:T(8,128)(2,1)} %param.15) | copy-start | bytes 49156
  261.7 20.3 %all-to-all-start.3 = ((bf16[8,16,512]{2,0,1:T(8,128)(2,1)}), bf16[8,16,512]{2,0,1:T(8,128)(2,1)S(1)}, u32[]{:S(2)}, u32[]{:S(2)}) async-start(bf16[8,16,512]{2,0,1:T(8,128)(2,1)} %bitcast.22), calls=%async_computation.3 | async-start | bytes 262144 | tf_op jit(solution)/shard_map/all_to_all | solution.py:162
  282.0 13.9 %all-to-all-start.4 = ((bf16[8,16,512]{2,0,1:T(8,128)(2,1)}), bf16[8,16,512]{2,0,1:T(8,128)(2,1)S(1)}, u32[]{:S(2)}, u32[]{:S(2)}) async-start(bf16[8,16,512]{2,0,1:T(8,128)(2,1)} %copy.83), calls=%async_computation.4 | async-start | bytes 262144 | tf_op jit(solution)/shard_map/all_to_all | solution.py:163
  288.0 88.5 %reduce-scatter.2.cloned.1.call-start = ((), (), s32[]{:S(2)}) async-start(), calls=%async_computation.7 | async-start | bytes 4456448 | tf_op jit(solution)/shard_map/reduce_scatter | solution.py:165
  303.7 0.7 copy-start.18
  303.7 73.9 %copy-start.10 = (f32[8192]{0:T(1024)S(1)}, f32[8192]{0:T(1024)}, u32[]{:S(2)}) copy-start(f32[8192]{0:T(1024)} %param.19) | copy-start | bytes 98308
Sparse Core Ops, SparseCore 0:
  10.2 44.0 all-gather.1
  303.8 72.5 reduce-scatter.1
where the time goes:
time: 387 us; the launch traced here: 386 us
  blocking collectives  122 us (32%)
  waiting for transfers between devices  119 us (31%)
  matrix products  41.9 us (11%)
  local copies, waits for them, and re-layouts  36.2 us (9%)
  other arithmetic  26.8 us (7%)
  starting transfers between devices  25.5 us (7%)
  between operations  14.8 us (4%)
    all_gather x1, blocking collectives, body(): lax.all_gather(tree_key_heads, 'ctx', axis=0, tiled=True)  86.5 us
    reduce_scatter x1, waiting for transfers between devices, body(): lax.psum_scatter(jnp.dot(embed_cols, fc_embed, preferred_element_type=jnp...  70.5 us
    all_gather x1, waiting for transfers between devices, body(): lax.all_gather(queries, 'ctx', axis=0, tiled=True)  46.4 us
    all_gather x1, blocking collectives, body(): lax.all_gather(tree_value_heads, 'ctx', axis=0, tiled=True)  35.8 us
    dot_general x8, matrix products, prefix_partial(): jnp.dot(weights.astype(jnp.bfloat16), group_v, preferred_element_type=jnp...  14.8 us
    reduce_sum x1, other arithmetic, body(): jnp.sum(piece_num.reshape(ctx_size, owned_rows, QUERY_HEADS, HEAD_WIDTH)...  13.1 us
    dot_general x8, matrix products, prefix_partial(): jnp.einsum('qd,kd->qk', group_q, group_k, preferred_element_type=jnp.floa...  10.8 us
    unnamed x50, local copies, waits for them, and re-layouts  9.73 us
  transfers between devices with their start and end apart: 7, of which 3 were waited for; matrix products, arithmetic and copies ran while one was open for 12% of the time, Pallas kernels for 0%

commit v1 on v0

v1 whole, which is shorter than its diff:
```python
import functools

import jax
import jax.numpy as jnp
from jax import lax
from jax.experimental import pallas as pl
from jax.experimental.pallas import tpu as pltpu
from jax.sharding import PartitionSpec as P

QUERY_HEADS = 64
KEY_HEADS = 8
HEAD_WIDTH = 128
GROUP = QUERY_HEADS // KEY_HEADS
PATH_ROWS = 7
negative_fill = -1e30


def round_up(value, step):
    return (value + step - 1) // step * step


def ancestors(parents):
    nodes = parents.shape[1]
    column = jnp.arange(nodes, dtype=jnp.int32)
    upward = parents[:, :, None] == column[None, None, :]
    closure = (upward | jnp.eye(nodes, dtype=bool)[None]).astype(jnp.bfloat16)
    for repeat in range((PATH_ROWS - 1).bit_length()):
        counts = jnp.einsum("tij,tjk->tik", closure, closure, preferred_element_type=jnp.float32)
        closure = jnp.minimum(counts, 1.0).astype(jnp.bfloat16)
    return closure


def attention_kernel(block, q_ref, k_ref, v_ref, tk_ref, tv_ref, mask_ref, num_ref, stat_ref):
    scale_factor = HEAD_WIDTH ** (-0.5)
    query_rows = q_ref.shape[0]
    tile = min(256, query_rows)
    blocks = k_ref.shape[0] // block

    @pl.loop(0, query_rows // tile)
    def _(t):
        rows = pl.ds(pl.multiple_of(t * tile, tile), tile)
        q = q_ref[rows, :]

        def step(carry, k, v, mask):
            top, den, num = carry
            s = lax.dot_general(q, k, (((1,), (1,)), ((), ())), preferred_element_type=jnp.float32)
            s = s * scale_factor
            if mask is not None:
                s = jnp.where(mask > 0.5, s, negative_fill)
            new_top = jnp.maximum(top, jnp.max(s, axis=1, keepdims=True))
            factor = jnp.exp(top - new_top)
            w = jnp.exp(s - new_top)
            den = den * factor + jnp.sum(w, axis=1, keepdims=True)
            num = num * factor + jnp.dot(
                w.astype(jnp.bfloat16), v, preferred_element_type=jnp.float32
            )
            return new_top, den, num

        def key_block(b, carry):
            keys = pl.ds(pl.multiple_of(b * block, block), block)
            return step(carry, k_ref[keys, :], v_ref[keys, :], None)

        carry = (
            jnp.full((tile, 1), negative_fill, jnp.float32),
            jnp.zeros((tile, 1), jnp.float32),
            jnp.zeros((tile, HEAD_WIDTH), jnp.float32),
        )
        carry = lax.fori_loop(0, blocks, key_block, carry)
        mask = mask_ref[pl.ds(pl.multiple_of(t * (tile // GROUP), tile // GROUP), tile // GROUP), :]
        mask = jnp.broadcast_to(mask[:, None, :], (tile // GROUP, GROUP, mask.shape[1]))
        top, den, num = step(carry, tk_ref[...], tv_ref[...], mask.reshape(tile, mask.shape[2]))
        num_ref[rows, :] = num
        lane = lax.broadcasted_iota(jnp.int32, (tile, HEAD_WIDTH), 1)
        stat_ref[rows, :] = jnp.where(lane < HEAD_WIDTH // 2, top, den)


def body(
    queries,
    prefix_key_heads,
    prefix_value_heads,
    tree_key_heads,
    tree_value_heads,
    token_embed,
    fc_embed,
    fc_feature,
    draft_gain,
    parents,
    accepted,
):
    tree_count, node_count = parents.shape
    owned = queries.shape[0]
    positions = prefix_key_heads.shape[0]
    every_row = tree_count * node_count
    n = lax.axis_size("ctx")
    me = lax.axis_index("ctx")
    members = n // KEY_HEADS
    part_heads = GROUP // members
    own_cols = part_heads * HEAD_WIDTH

    across = [[j * members + m for j in range(KEY_HEADS)] for m in range(members)]
    beside = [[j * members + m for m in range(members)] for j in range(KEY_HEADS)]
    kv = jnp.concatenate(
        [
            x.reshape(positions, KEY_HEADS, HEAD_WIDTH).transpose(1, 0, 2)[:, None]
            for x in (prefix_key_heads, prefix_value_heads)
        ],
        axis=1,
    )
    kv = lax.all_to_all(kv, "ctx", 0, 0, axis_index_groups=across, tiled=True)

    def heads(x, count):
        return x.reshape(owned, KEY_HEADS, count, HEAD_WIDTH).transpose(1, 0, 2, 3).reshape(
            KEY_HEADS, owned * count, HEAD_WIDTH
        )

    shared = jnp.concatenate(
        [heads(queries, GROUP), heads(tree_key_heads, 1), heads(tree_value_heads, 1)], axis=1
    )
    shared = jnp.repeat(shared, members, axis=0)
    embed = token_embed.reshape(owned, n, part_heads, HEAD_WIDTH).transpose(1, 0, 2, 3)
    embed = embed.reshape(n, owned * part_heads, HEAD_WIDTH)
    small = lax.all_to_all(
        jnp.concatenate([shared, embed], axis=1), "ctx", 0, 0, tiled=True
    )
    cut = [owned * GROUP, owned * (GROUP + 1), owned * (GROUP + 2)]
    q, tk, tv, embed = jnp.split(small, cut, axis=1)
    q = q.reshape(every_row * GROUP, HEAD_WIDTH)
    tk = tk.reshape(every_row, HEAD_WIDTH)
    tv = tv.reshape(every_row, HEAD_WIDTH)
    embed_cols = embed.reshape(every_row, own_cols)

    closure = ancestors(parents)
    own_tree = jnp.arange(every_row, dtype=jnp.int32) // node_count
    allowed = jnp.tile(closure.reshape(every_row, node_count).astype(jnp.float32), (1, tree_count))
    allowed = jnp.where(
        (own_tree[:, None] == own_tree[None, :]) & (me % members == 0), allowed, 0.0
    )
    chosen = accepted[:, None] == jnp.arange(node_count, dtype=jnp.int32)[None, :]
    on_path = jnp.max(
        jnp.where(chosen[:, :, None], closure.astype(jnp.float32), 0.0), axis=1
    ).reshape(every_row)
    row_index = jnp.arange(every_row, dtype=jnp.int32)
    rank = jnp.sum(
        jnp.where(row_index[:, None] < row_index[None, :], on_path[:, None], 0.0), axis=0
    ).astype(jnp.int32)
    slots = round_up(tree_count * PATH_ROWS, 16)
    pick = (
        (rank[None, :] == jnp.arange(slots, dtype=jnp.int32)[:, None]) & (on_path[None, :] > 0.5)
    ).astype(jnp.bfloat16)

    num, stat = pl.pallas_call(
        functools.partial(attention_kernel, positions),
        out_shape=[jax.ShapeDtypeStruct((every_row * GROUP, HEAD_WIDTH), jnp.float32)] * 2,
        compiler_params=pltpu.CompilerParams(vmem_limit_bytes=48 * 1024 * 1024),
    )(
        q,
        kv[:, 0].reshape(-1, HEAD_WIDTH),
        kv[:, 1].reshape(-1, HEAD_WIDTH),
        tk,
        tv,
        allowed,
    )
    both = jnp.concatenate([num, stat], axis=1).reshape(
        every_row, members, part_heads, 2 * HEAD_WIDTH
    )
    both = lax.all_to_all(
        both.transpose(1, 0, 2, 3), "ctx", 0, 0, axis_index_groups=beside, tiled=True
    )
    num = both[..., :HEAD_WIDTH]
    top = both[..., HEAD_WIDTH]
    den = both[..., 2 * HEAD_WIDTH - 1]
    factor = jnp.exp(top - jnp.max(top, axis=0)[None])
    num = jnp.sum(num * factor[..., None], axis=0)
    den = jnp.sum(den * factor, axis=0)
    part = (num / den[..., None]).reshape(every_row, own_cols).astype(jnp.bfloat16)
    attended = lax.all_to_all(part, "ctx", 0, 1, tiled=True)

    def compact(x):
        return jnp.dot(pick, x, preferred_element_type=jnp.float32).astype(jnp.bfloat16)

    joined = jnp.dot(compact(embed_cols), fc_embed, preferred_element_type=jnp.float32)
    joined = joined + jnp.dot(compact(part), fc_feature, preferred_element_type=jnp.float32)
    joined = lax.psum(joined, "ctx")
    mean_square = jnp.mean(joined * joined, axis=1, keepdims=True)
    normed = (joined * lax.rsqrt(mean_square + 1e-06) * draft_gain[None, :]).astype(jnp.bfloat16)
    own_pick = lax.dynamic_slice_in_dim(pick, me * owned, owned, 1)
    draft_input = jnp.einsum(
        "sr,sd->rd", own_pick, normed, preferred_element_type=jnp.float32
    ).astype(jnp.bfloat16)
    return (attended, draft_input)


def solution(mesh):
    placed = (
        P(("groups", "ctx"), None),
        P(("groups", "ctx"), None),
        P(("groups", "ctx"), None),
        P(("groups", "ctx"), None),
        P(("groups", "ctx"), None),
        P(("groups", "ctx"), None),
        P("ctx", None),
        P("ctx", None),
        P(),
        P("groups", None),
        P("groups"),
    )
    return jax.shard_map(
        body,
        mesh=mesh,
        in_specs=placed,
        out_specs=(P(("groups", "ctx"), None), P(("groups", "ctx"), None)),
        check_vma=False,
    )
```

time: 387 us -> 214 us (0.55)
  blocking collectives: 122 us -> 4.58 us
  matrix products: 41.9 us -> 12.7 us
  local copies, waits for them, and re-layouts: 36.2 us -> 13.9 us
  other arithmetic: 26.8 us -> 4.89 us
  Pallas kernels: 0 us -> 17.3 us
  waiting for transfers between devices: 119 us -> 131 us
  starting transfers between devices: 25.5 us -> 15 us
    all_gather x2 -> x0, blocking collectives: 122 us -> none  [the longest x1 86.5 us: body(): lax.all_gather(tree_key_heads, 'ctx', axis=0, tiled=True)]
    psum x0 -> x1, waiting for transfers between devices: none -> 76.7 us  [body(): joined = lax.psum(joined, 'ctx')]
    reduce_scatter x1 -> x0, waiting for transfers between devices: 70.5 us -> none  [body(): lax.psum_scatter(jnp.dot(embed_cols, fc_embed, preferred_element_type=jnp...]
    all_to_all x5 -> x3, waiting for transfers between devices: 1.1 us -> 54 us  [the longest x1 40 us: body(): kv = lax.all_to_all(kv, 'ctx', 0, 0, axis_index_groups=across, tiled=True)]
    all_gather x1 -> x0, waiting for transfers between devices: 46.4 us -> none  [body(): lax.all_gather(queries, 'ctx', axis=0, tiled=True)]
    dot_general x27 -> x5, matrix products: 41.9 us -> 12.7 us  [the longest x1 5.52 us: body(): jnp.dot(compact(part), fc_feature, preferred_element_type=jnp.float32)]
    reduce_sum x12 -> x4, other arithmetic: 19.9 us -> 1.48 us  [the longest x1 1.22 us: body(): mean_square = jnp.mean(joined * joined, axis=1, keepdims=True)]
    pallas_call x0 -> x1, Pallas kernels: none -> 17.3 us  [body(): pl.pallas_call(functools.partial(attention_kernel, positions), out_shape=...]
  transfers between devices with their start and end apart: 7 -> 4, of which waited for: 3 -> 4; matrix products, arithmetic and copies ran while one was open for 12% -> 8% of each run, Pallas kernels for 0% -> 0%
where the time goes in v1:
time: 214 us; the launch traced here: 213 us
  waiting for transfers between devices  131 us (61%)
  Pallas kernels  17.3 us (8%)
  starting transfers between devices  15 us (7%)
  between operations  14.3 us (7%)
  local copies, waits for them, and re-layouts  13.9 us (6%)
  matrix products  12.7 us (6%)
  other arithmetic  4.89 us (2%)
  blocking collectives  4.58 us (2%)
    psum x1, waiting for transfers between devices, body(): joined = lax.psum(joined, 'ctx')  76.7 us
    all_to_all x1, waiting for transfers between devices, body(): kv = lax.all_to_all(kv, 'ctx', 0, 0, axis_index_groups=across, tiled=True)  40 us
    pallas_call x1, Pallas kernels, body(): pl.pallas_call(functools.partial(attention_kernel, positions), out_shape=...  17.3 us
    all_to_all x1, waiting for transfers between devices, body(): attended = lax.all_to_all(part, 'ctx', 0, 1, tiled=True)  8.31 us
    all_to_all x1, starting transfers between devices, body(): lax.all_to_all(jnp.concatenate([shared, embed], axis=1), 'ctx', 0, 0, til...  7.43 us
    all_to_all x1, waiting for transfers between devices, body(): lax.all_to_all(jnp.concatenate([shared, embed], axis=1), 'ctx', 0, 0, til...  5.67 us
    dot_general x1, matrix products, body(): jnp.dot(compact(part), fc_feature, preferred_element_type=jnp.float32)  5.52 us
    dot_general x1, matrix products, body(): jnp.dot(compact(embed_cols), fc_embed, preferred_element_type=jnp.float32)  4.68 us
  transfers between devices with their start and end apart: 4, of which 4 were waited for; matrix products, arithmetic and copies ran while one was open for 8% of the time, Pallas kernels for 0%

profile of v1, /device:TPU:0, one launch (start us, length us, event | category | flops | bytes accessed | tf_op | source)
XLA Modules:
  0.0 213.4 jit_solution(2631179275613395084)
XLA Ops:
  7.2 1.0 copy.50
  8.1 0.9 copy_bitcast_fusion
  9.1 0.8 pad_maximum_fusion.3
  9.9 0.8 pad_maximum_fusion.2
  10.7 7.4 %all-to-all-start = ((bf16[16,112,128]{2,1,0:T(8,128)(2,1)}), bf16[16,112,128]{2,1,0:T(8,128)(2,1)}, u32[]{:S(2)}, u32[]{:S(2)}) async-start(bf16[16,112,128]{2,1,0:T(8,128)(2,1)} %pad_maximum_fusion.2), calls=%async_computation | async-start | bytes 917504 | tf_op jit(solution)/shard_map/all_to_all | solution.py:122
  18.1 0.0 copy-start.2
  18.1 1.5 copy.52
  19.6 2.3 %copy.51 = bf16[512,1024]{0,1:T(8,128)(2,1)} copy(bf16[512,1024]{1,0:T(8,128)(2,1)} %param.12) | data formatting | bytes 2097152 | tf_op args[1]
  21.9 1.4 pad_maximum_fusion
  23.3 2.4 %copy.53 = bf16[8,2,512,128]{3,2,1,0:T(8,128)(2,1)} copy(bf16[8,2,512,128]{2,3,0,1:T(8,128)(2,1)S(1)} %pad_maximum_fusion) | data formatting | bytes 4194304 | tf_op jit(solution)/shard_map/concatenate | solution.py:102
  25.7 5.7 %all-to-all-done = bf16[16,112,128]{2,1,0:T(8,128)(2,1)} async-done(((bf16[16,112,128]{2,1,0:T(8,128)(2,1)}), bf16[16,112,128]{2,1,0:T(8,128)(2,1)}, u32[]{:S(2)}, u32[]{:S(2)}) %all-to-all-start) | async-done | bytes 458784 | tf_op jit(solution)/shard_map/all_to_all | solution.py:122
  31.4 3.8 %all-to-all-start.1 = ((bf16[8,2,512,128]{3,2,1,0:T(8,128)(2,1)}), bf16[8,2,512,128]{3,2,1,0:T(8,128)(2,1)S(1)}, u32[]{:S(2)}, u32[]{:S(2)}) async-start(bf16[8,2,512,128]{3,2,1,0:T(8,128)(2,1)} %copy.53), calls=%async_computation.1 | async-start | bytes 4194304 | tf_op jit(solution)/shard_map/all_to_all | solution.py:109
  35.2 0.0 all-reduce.2.cloned.1.call-start
  35.3 0.1 iota_compare_fusion.4
  35.4 0.4 fusion.1
  35.7 0.2 select_reduce_fusion.1
  35.9 0.1 copy.54
  36.0 0.1 copy.55
  36.1 0.1 broadcast_in_dim.60
  36.2 0.1 select_reduce_fusion
  36.3 0.1 and_select_fusion.mask_ref
  36.4 0.9 split.19
  37.3 0.1 reshape.167
  37.4 1.0 split.16
  38.4 0.8 slice_bitcast_fusion
  39.2 4.7 %fusion.4 = f32[16,8192]{1,0:T(8,128)S(1)} fusion(bf16[512,8192]{1,0:T(8,128)(2,1)} %param.17, bf16[128,512]{1,0:T(8,128)(2,1)S(1)} %reshape.167, s32[128]{0:T(128)S(1)} %convert_element_type.61, pred[128]{0:T(512)(128)(4,1)S(1)} %broadcast_compare_fusion), kind=kOutput, calls=%fused_computation.12 | convolution fusion | flops 136327168 | bytes 9044608 | tf_op jit(solution)/shard_map/dot_general | solution.py:181
  43.9 40.0 %all-to-all-done.1 = bf16[8,2,512,128]{3,2,1,0:T(8,128)(2,1)S(1)} async-done(((bf16[8,2,512,128]{3,2,1,0:T(8,128)(2,1)}), bf16[8,2,512,128]{3,2,1,0:T(8,128)(2,1)S(1)}, u32[]{:S(2)}, u32[]{:S(2)}) %all-to-all-start.1) | async-done | bytes 2097184 | tf_op jit(solution)/shard_map/all_to_all | solution.py:109
  83.9 0.1 fusion.29
  84.0 17.3 %shard_map.122 = (f32[1024,128]{1,0:T(8,128)S(1)}, f32[1024,128]{1,0:T(8,128)S(1)}) custom-call(bf16[1024,128]{1,0:T(8,128)(2,1)S(1)} %bitcast.79, bf16[4096,128]{1,0:T(8,128)(2,1)S(1)} %bitcast.78, bf16[4096,128]{1,0:T(8,128)(2,1)S(1)} %bitcast.77, bf16[128,128]{1,0:T(8,128)(2,1)S(1)} %get-tuple-element.9.tk_ref, ...), custom_call_target="tpu_custom_call" | custom-call | tf_op jit(solution)/shard_map/pallas_call | solution.py:151
  101.4 0.1 pad_maximum_fusion.1
  101.5 0.3 reshape.166
  101.8 0.0 copy-start
  101.8 0.6 copy.56
  102.4 4.6 %all_to_all.31 = f32[2,128,4,256]{1,2,3,0:T(4,128)S(1)} all-to-all(f32[2,128,4,256]{1,2,3,0:T(4,128)S(1)} %bitcast.80), channel_id=1, replica_groups={{0,1},{2,3},{4,5},{6,7},{8,9},{10,11},{12,13},{14,15},{16,17},{18,19},{..., dimensions={0} | all-to-all | bytes 2097152 | tf_op jit(solution)/shard_map/all_to_all | solution.py:166
  107.0 0.1 fusion.5
  107.1 0.1 copy.59
  107.3 0.1 divide_convert_fusion
  107.4 0.1 copy.61
  107.6 5.5 %convolution_add_fusion = f32[16,8192]{1,0:T(8,128)} fusion(f32[16,8192]{1,0:T(8,128)S(1)} %fusion.4, bf16[512,8192]{1,0:T(8,128)(2,1)} %param.18, bf16[128,512]{0,1:T(8,128)(2,1)S(1)} %bitcast.84, s32[128]{0:T(128)S(1)} %convert_element_type.61, pred[128]{0:T(512)(128)(4,1)S(1)} %broadcast_compare_fusion), kind=kOutput, calls=%fused_computation | convolution fusion | flops 136458240 | bytes 9568896 | tf_op jit(solution)/shard_map/dot_general | solution.py:182
  113.1 0.0 all-reduce.2.cloned.1.call-update
  113.1 0.1 copy.60
  113.2 0.7 convert_element_type.59
  113.9 3.7 %all-to-all-start.3 = ((bf16[16,8,512]{2,1,0:T(8,128)(2,1)}), bf16[16,8,512]{2,1,0:T(8,128)(2,1)S(1)}, u32[]{:S(2)}, u32[]{:S(2)}) async-start(bf16[16,8,512]{2,1,0:T(8,128)(2,1)} %convert_element_type.59), calls=%async_computation.3 | async-start | bytes 262144 | tf_op jit(solution)/shard_map/all_to_all | solution.py:176
  117.7 8.3 %all-to-all-done.3 = bf16[16,8,512]{2,1,0:T(8,128)(2,1)S(1)} async-done(((bf16[16,8,512]{2,1,0:T(8,128)(2,1)}), bf16[16,8,512]{2,1,0:T(8,128)(2,1)S(1)}, u32[]{:S(2)}, u32[]{:S(2)}) %all-to-all-start.3) | async-done | bytes 131104 | tf_op jit(solution)/shard_map/all_to_all | solution.py:176
  126.0 76.7 %all-reduce.2.cloned.1.call-done = f32[16,8192]{1,0:T(8,128)} async-done(((f32[16,8192]{1,0:T(8,128)}), f32[16,8192]{1,0:T(8,128)}) %all-reduce.2.cloned.1.call-update) | async-done | bytes 524304 | tf_op jit(solution)/shard_map/psum | solution.py:183
  202.7 1.2 multiply_reduce_fusion
  203.9 2.0 convolution_convert_fusion
  205.9 0.7 copy.70
  (15 shorter events, 0.2 us)
Async XLA Ops:
  10.7 20.7 %all-to-all-start = ((bf16[16,112,128]{2,1,0:T(8,128)(2,1)}), bf16[16,112,128]{2,1,0:T(8,128)(2,1)}, u32[]{:S(2)}, u32[]{:S(2)}) async-start(bf16[16,112,128]{2,1,0:T(8,128)(2,1)} %pad_maximum_fusion.2), calls=%async_computation | async-start | bytes 917504 | tf_op jit(solution)/shard_map/all_to_all | solution.py:122
  18.1 17.2 %copy-start.2 = (s32[2]{0:T(128)S(1)}, s32[2]{0:T(128)}, u32[]{:S(2)}) copy-start(s32[2]{0:T(128)} %param.21) | copy-start | bytes 28
  18.1 17.2 %copy-start.1 = (s32[2,64]{1,0:T(2,128)S(1)}, s32[2,64]{1,0:T(2,128)}, u32[]{:S(2)}) copy-start(s32[2,64]{1,0:T(2,128)} %param.20) | copy-start | bytes 1540
  31.4 52.5 %all-to-all-start.1 = ((bf16[8,2,512,128]{3,2,1,0:T(8,128)(2,1)}), bf16[8,2,512,128]{3,2,1,0:T(8,128)(2,1)S(1)}, u32[]{:S(2)}, u32[]{:S(2)}) async-start(bf16[8,2,512,128]{3,2,1,0:T(8,128)(2,1)} %copy.53), calls=%async_computation.1 | async-start | bytes 4194304 | tf_op jit(solution)/shard_map/all_to_all | solution.py:109
  35.2 167.5 %all-reduce.2.cloned.1.call-start = ((), (), s32[]{:S(2)}) async-start(), calls=%async_computation.4 | async-start | bytes 1048576 | tf_op jit(solution)/shard_map/psum | solution.py:183
  101.8 102.2 %copy-start = (f32[8192]{0:T(1024)S(1)}, f32[8192]{0:T(1024)}, u32[]{:S(2)}) copy-start(f32[8192]{0:T(1024)} %param.19) | copy-start | bytes 98308
  113.9 12.1 %all-to-all-start.3 = ((bf16[16,8,512]{2,1,0:T(8,128)(2,1)}), bf16[16,8,512]{2,1,0:T(8,128)(2,1)S(1)}, u32[]{:S(2)}, u32[]{:S(2)}) async-start(bf16[16,8,512]{2,1,0:T(8,128)(2,1)} %convert_element_type.59), calls=%async_computation.3 | async-start | bytes 262144 | tf_op jit(solution)/shard_map/all_to_all | solution.py:176
Sparse Core Ops, SparseCore 0:
  113.2 89.4 all-reduce.1

commit v2 on v1

v2 whole, which is shorter than its diff:
```python
import functools

import jax
import jax.numpy as jnp
from jax import lax
from jax.experimental import pallas as pl
from jax.experimental.pallas import tpu as pltpu
from jax.sharding import PartitionSpec as P

QUERY_HEADS = 64
KEY_HEADS = 8
HEAD_WIDTH = 128
GROUP = QUERY_HEADS // KEY_HEADS
PATH_ROWS = 7
negative_fill = -1e30


def round_up(value, step):
    return (value + step - 1) // step * step


def ancestors(parents):
    nodes = parents.shape[1]
    column = jnp.arange(nodes, dtype=jnp.int32)
    upward = parents[:, :, None] == column[None, None, :]
    closure = (upward | jnp.eye(nodes, dtype=bool)[None]).astype(jnp.bfloat16)
    for repeat in range((PATH_ROWS - 1).bit_length()):
        counts = jnp.einsum("tij,tjk->tik", closure, closure, preferred_element_type=jnp.float32)
        closure = jnp.minimum(counts, 1.0).astype(jnp.bfloat16)
    return closure


def greet(n, me):
    barrier = pltpu.get_barrier_semaphore()

    @pl.loop(1, n)
    def _(r):
        pl.semaphore_signal(
            barrier, inc=1, device_id={"ctx": lax.rem(me + r, n)}, device_id_type=pl.DeviceIdType.MESH
        )

    pl.semaphore_wait(barrier, n - 1)


def push(source, target, send_sem, recv_sem, device):
    return pltpu.make_async_remote_copy(
        src_ref=source,
        dst_ref=target,
        send_sem=send_sem,
        recv_sem=recv_sem,
        device_id={"ctx": device},
        device_id_type=pl.DeviceIdType.MESH,
    )


def attention_kernel(
    n,
    q_rows,
    tree_rows,
    small_ref,
    k_ref,
    v_ref,
    mask_ref,
    num_ref,
    stat_ref,
    embed_ref,
    small,
    keys,
    values,
    tree_k,
    tree_v,
    top_ref,
    den_ref,
    small_send,
    small_recv,
    kv_send,
    kv_recv,
    local_sem,
):
    scale_factor = HEAD_WIDTH ** (-0.5)
    members = n // KEY_HEADS
    me = lax.axis_index("ctx")
    mine = me // members
    member = lax.rem(me, members)
    greet(n, me)

    def small_copy(r):
        to = lax.rem(me + r, n)
        return push(small_ref.at[to], small.at[me], small_send.at[r], small_recv.at[me], to)

    def head_of(ref, j):
        return ref.at[:, pl.ds(pl.multiple_of(j * HEAD_WIDTH, HEAD_WIDTH), HEAD_WIDTH)]

    def kv_copy(r, which):
        j = lax.rem(mine + r, KEY_HEADS)
        source, target = ((k_ref, keys), (v_ref, values))[which]
        return push(
            head_of(source, j),
            target.at[mine],
            kv_send.at[which, r],
            kv_recv.at[which, mine],
            j * members + member,
        )

    @pl.loop(1, n)
    def _(r):
        small_copy(r).start()

    @pl.loop(1, KEY_HEADS)
    def _(r):
        kv_copy(r, 0).start()
        kv_copy(r, 1).start()

    own = [
        pltpu.make_async_copy(small_ref.at[me], small.at[me], local_sem.at[0]),
        pltpu.make_async_copy(head_of(k_ref, mine), keys.at[mine], local_sem.at[1]),
        pltpu.make_async_copy(head_of(v_ref, mine), values.at[mine], local_sem.at[2]),
    ]
    for copy in own:
        copy.start()
    for copy in own:
        copy.wait()

    @pl.loop(1, n)
    def _(r):
        source = lax.rem(me - r + n, n)
        push(
            small_ref.at[source], small.at[source], small_send.at[r], small_recv.at[source], source
        ).wait_recv()

    stack = max(1, 256 // q_rows)
    tile = stack * q_rows
    rows_of_tile = tile // GROUP

    def step(t, k, v, mask, first):
        rows = pl.ds(pl.multiple_of(t * tile, tile), tile)
        q = small[pl.ds(t * stack, stack), 0:q_rows, :].reshape(tile, HEAD_WIDTH)
        s = lax.dot_general(q, k, (((1,), (1,)), ((), ())), preferred_element_type=jnp.float32)
        s = s * scale_factor
        if mask is not None:
            s = jnp.where(mask > 0.5, s, negative_fill)
        highest_here = jnp.max(s, axis=1, keepdims=True)
        if first:
            new_top = highest_here
        else:
            top = top_ref[rows, :]
            new_top = jnp.maximum(top, highest_here)
            factor = jnp.exp(top - new_top)
        w = jnp.exp(s - new_top)
        den = jnp.sum(w, axis=1, keepdims=True)
        num = jnp.dot(w.astype(jnp.bfloat16), v, preferred_element_type=jnp.float32)
        if not first:
            den = den + den_ref[rows, :] * factor
            num = num + num_ref[rows, :] * factor
        top_ref[rows, :] = new_top
        den_ref[rows, :] = den
        num_ref[rows, :] = num

    tree_k[...] = small[:, q_rows : q_rows + tree_rows, :].reshape(tree_k.shape)
    tree_v[...] = small[:, q_rows + tree_rows : q_rows + 2 * tree_rows, :].reshape(tree_v.shape)
    embed_ref[...] = small[:, q_rows + 2 * tree_rows :, :]
    tiles = n // stack

    @pl.loop(0, tiles)
    def _(t):
        start = pl.multiple_of(t * rows_of_tile, rows_of_tile)
        mask = mask_ref[pl.ds(start, rows_of_tile), :]
        mask = jnp.broadcast_to(mask[:, None, :], (rows_of_tile, GROUP, mask.shape[1]))
        step(t, tree_k[...], tree_v[...], mask.reshape(tile, mask.shape[2]), True)

    @pl.loop(0, KEY_HEADS)
    def _(r):
        j = lax.rem(mine - r + KEY_HEADS, KEY_HEADS)

        @pl.when(r > 0)
        def _():
            source = j * members + member
            for which, target in ((0, keys), (1, values)):
                push(
                    target.at[j], target.at[j], kv_send.at[which, r], kv_recv.at[which, j], source
                ).wait_recv()

        @pl.loop(0, tiles)
        def _(t):
            step(t, keys[j], values[j], None, False)

    lane = lax.broadcasted_iota(jnp.int32, stat_ref.shape, 1)
    stat_ref[...] = jnp.where(lane < HEAD_WIDTH // 2, top_ref[...], den_ref[...])

    @pl.loop(1, n)
    def _(r):
        small_copy(r).wait_send()

    @pl.loop(1, KEY_HEADS)
    def _(r):
        kv_copy(r, 0).wait_send()
        kv_copy(r, 1).wait_send()


def join_kernel(
    n, joined_ref, gain_ref, pick_ref, out_ref, pieces, sums, send_a, recv_a, send_b, recv_b
):
    me = lax.axis_index("ctx")
    width = pieces.shape[2]
    greet(n, me)

    def columns(d):
        return joined_ref.at[:, pl.ds(pl.multiple_of(d * width, width), width)]

    def piece(r):
        to = lax.rem(me + r, n)
        return push(columns(to), pieces.at[me], send_a.at[r], recv_a.at[me], to)

    def total(r):
        to = lax.rem(me + r, n)
        return push(sums.at[me], sums.at[me], send_b.at[r], recv_b.at[me], to)

    @pl.loop(1, n)
    def _(r):
        piece(r).start()

    pieces[me] = joined_ref[:, pl.ds(pl.multiple_of(me * width, width), width)]

    @pl.loop(1, n)
    def _(r):
        source = lax.rem(me - r + n, n)
        push(pieces.at[source], pieces.at[source], send_a.at[r], recv_a.at[source], source).wait_recv()

    sums[me] = jnp.sum(pieces[...], axis=0)

    @pl.loop(1, n)
    def _(r):
        total(r).start()

    @pl.loop(1, n)
    def _(r):
        source = lax.rem(me - r + n, n)
        push(sums.at[source], sums.at[source], send_b.at[r], recv_b.at[source], source).wait_recv()

    joined = sums[...]
    squares = jnp.sum(jnp.sum(joined * joined, axis=0), axis=1, keepdims=True)
    inverse = lax.rsqrt(squares / (n * width) + 1e-06)
    for d in range(n):
        normed = sums[d] * inverse * gain_ref[:, d * width : (d + 1) * width]
        out_ref[:, d * width : (d + 1) * width] = jnp.dot(
            pick_ref[...], normed.astype(jnp.bfloat16), preferred_element_type=jnp.float32
        ).astype(jnp.bfloat16)

    @pl.loop(1, n)
    def _(r):
        piece(r).wait_send()
        total(r).wait_send()


def body(
    queries,
    prefix_key_heads,
    prefix_value_heads,
    tree_key_heads,
    tree_value_heads,
    token_embed,
    fc_embed,
    fc_feature,
    draft_gain,
    parents,
    accepted,
):
    tree_count, node_count = parents.shape
    owned = queries.shape[0]
    positions = prefix_key_heads.shape[0]
    every_row = tree_count * node_count
    n = lax.axis_size("ctx")
    me = lax.axis_index("ctx")
    members = n // KEY_HEADS
    part_heads = GROUP // members
    own_cols = part_heads * HEAD_WIDTH

    beside = [[j * members + m for m in range(members)] for j in range(KEY_HEADS)]
    q_rows = owned * GROUP
    tree_rows = round_up(owned, 16)

    def pieces_of(x, parts, count, rows):
        x = x.reshape(owned, parts, count, HEAD_WIDTH).transpose(1, 0, 2, 3)
        x = x.reshape(parts, owned * count, HEAD_WIDTH)
        return jnp.pad(x, ((0, 0), (0, rows - owned * count), (0, 0)))

    shared = jnp.concatenate(
        [
            pieces_of(queries, KEY_HEADS, GROUP, q_rows),
            pieces_of(tree_key_heads, KEY_HEADS, 1, tree_rows),
            pieces_of(tree_value_heads, KEY_HEADS, 1, tree_rows),
        ],
        axis=1,
    )
    embed_rows = round_up(owned * part_heads, 16)
    small = jnp.concatenate(
        [
            jnp.repeat(shared, members, axis=0),
            pieces_of(token_embed, n, part_heads, embed_rows),
        ],
        axis=1,
    )

    closure = ancestors(parents)
    own_tree = jnp.arange(every_row, dtype=jnp.int32) // node_count
    allowed = jnp.tile(closure.reshape(every_row, node_count).astype(jnp.float32), (1, tree_count))
    allowed = jnp.where(
        (own_tree[:, None] == own_tree[None, :]) & (me % members == 0), allowed, 0.0
    )
    chosen = accepted[:, None] == jnp.arange(node_count, dtype=jnp.int32)[None, :]
    on_path = jnp.max(
        jnp.where(chosen[:, :, None], closure.astype(jnp.float32), 0.0), axis=1
    ).reshape(every_row)
    row_index = jnp.arange(every_row, dtype=jnp.int32)
    rank = jnp.sum(
        jnp.where(row_index[:, None] < row_index[None, :], on_path[:, None], 0.0), axis=0
    ).astype(jnp.int32)
    slots = round_up(tree_count * PATH_ROWS, 16)
    pick = (
        (rank[None, :] == jnp.arange(slots, dtype=jnp.int32)[:, None]) & (on_path[None, :] > 0.5)
    ).astype(jnp.bfloat16)

    allowed = jnp.pad(
        allowed.reshape(every_row, n, owned), ((0, 0), (0, 0), (0, tree_rows - owned))
    ).reshape(every_row, n * tree_rows)
    any_space = pl.BlockSpec(memory_space=pl.ANY)
    in_vmem = pl.BlockSpec(memory_space=pltpu.VMEM)
    num, stat, embed = pl.pallas_call(
        functools.partial(attention_kernel, n, q_rows, tree_rows),
        out_shape=[
            jax.ShapeDtypeStruct((every_row * GROUP, HEAD_WIDTH), jnp.float32),
            jax.ShapeDtypeStruct((every_row * GROUP, HEAD_WIDTH), jnp.float32),
            jax.ShapeDtypeStruct((n, embed_rows, HEAD_WIDTH), jnp.bfloat16),
        ],
        in_specs=[any_space] * 3 + [in_vmem],
        out_specs=[in_vmem] * 3,
        scratch_shapes=[
            pltpu.VMEM(small.shape, jnp.bfloat16),
            pltpu.VMEM((KEY_HEADS, positions, HEAD_WIDTH), jnp.bfloat16),
            pltpu.VMEM((KEY_HEADS, positions, HEAD_WIDTH), jnp.bfloat16),
            pltpu.VMEM((n * tree_rows, HEAD_WIDTH), jnp.bfloat16),
            pltpu.VMEM((n * tree_rows, HEAD_WIDTH), jnp.bfloat16),
            pltpu.VMEM((every_row * GROUP, 1), jnp.float32),
            pltpu.VMEM((every_row * GROUP, 1), jnp.float32),
            pltpu.SemaphoreType.DMA((n,)),
            pltpu.SemaphoreType.DMA((n,)),
            pltpu.SemaphoreType.DMA((2, KEY_HEADS)),
            pltpu.SemaphoreType.DMA((2, KEY_HEADS)),
            pltpu.SemaphoreType.DMA((3,)),
        ],
        compiler_params=pltpu.CompilerParams(
            collective_id=0, has_side_effects=True, vmem_limit_bytes=40 * 1024 * 1024
        ),
        cost_estimate=pl.CostEstimate(
            flops=4 * every_row * GROUP * positions * KEY_HEADS * HEAD_WIDTH,
            bytes_accessed=4 * prefix_key_heads.size,
            transcendentals=every_row * GROUP * positions * KEY_HEADS,
        ),
    )(small, prefix_key_heads, prefix_value_heads, allowed)
    embed_cols = embed[:, : owned * part_heads].reshape(every_row, own_cols)
    both = jnp.concatenate([num, stat], axis=1).reshape(
        every_row, members, part_heads, 2 * HEAD_WIDTH
    )
    both = lax.all_to_all(
        both.transpose(1, 0, 2, 3), "ctx", 0, 0, axis_index_groups=beside, tiled=True
    )
    num = both[..., :HEAD_WIDTH]
    top = both[..., HEAD_WIDTH]
    den = both[..., 2 * HEAD_WIDTH - 1]
    factor = jnp.exp(top - jnp.max(top, axis=0)[None])
    num = jnp.sum(num * factor[..., None], axis=0)
    den = jnp.sum(den * factor, axis=0)
    part = (num / den[..., None]).reshape(every_row, own_cols).astype(jnp.bfloat16)
    attended = lax.all_to_all(part, "ctx", 0, 1, tiled=True)

    def compact(x):
        return jnp.dot(pick, x, preferred_element_type=jnp.float32).astype(jnp.bfloat16)

    joined = jnp.dot(compact(embed_cols), fc_embed, preferred_element_type=jnp.float32)
    joined = joined + jnp.dot(compact(part), fc_feature, preferred_element_type=jnp.float32)
    own_pick = lax.dynamic_slice_in_dim(pick, me * owned, owned, 1).T
    width = joined.shape[1] // n
    draft_input = pl.pallas_call(
        functools.partial(join_kernel, n),
        out_shape=jax.ShapeDtypeStruct(token_embed.shape, jnp.bfloat16),
        in_specs=[in_vmem] * 3,
        out_specs=in_vmem,
        scratch_shapes=[
            pltpu.VMEM((n, slots, width), jnp.float32),
            pltpu.VMEM((n, slots, width), jnp.float32),
            pltpu.SemaphoreType.DMA((n,)),
            pltpu.SemaphoreType.DMA((n,)),
            pltpu.SemaphoreType.DMA((n,)),
            pltpu.SemaphoreType.DMA((n,)),
        ],
        compiler_params=pltpu.CompilerParams(
            collective_id=1, has_side_effects=True, vmem_limit_bytes=24 * 1024 * 1024
        ),
    )(joined, draft_gain[None, :], own_pick)
    return (attended, draft_input)


def solution(mesh):
    placed = (
        P(("groups", "ctx"), None),
        P(("groups", "ctx"), None),
        P(("groups", "ctx"), None),
        P(("groups", "ctx"), None),
        P(("groups", "ctx"), None),
        P(("groups", "ctx"), None),
        P("ctx", None),
        P("ctx", None),
        P(),
        P("groups", None),
        P("groups"),
    )
    return jax.shard_map(
        body,
        mesh=mesh,
        in_specs=placed,
        out_specs=(P(("groups", "ctx"), None), P(("groups", "ctx"), None)),
        check_vma=False,
    )
```

time: 214 us -> 134 us (0.63)
  the two profiles are of different devices: /device:TPU:0 before, /device:TPU:29 now
where the time goes in v2:
time: 134 us
  Pallas kernels  101 us (75%)
  matrix products  11 us (8%)
  local copies, waits for them, and re-layouts  8.03 us (6%)
  starting transfers between devices  6.03 us (4%)
  blocking collectives  5.07 us (4%)
  other arithmetic  2.26 us (2%)
    pallas_call x1, Pallas kernels, body(): pl.pallas_call(functools.partial(attention_kernel, n, q_rows, tree_rows),...  70.7 us
    pallas_call x1, Pallas kernels, body(): pl.pallas_call(functools.partial(join_kernel, n), out_shape=jax.ShapeDtyp...  29.9 us
    all_to_all x1, starting transfers between devices, body(): attended = lax.all_to_all(part, 'ctx', 0, 1, tiled=True)  6.03 us
    all_to_all x1, blocking collectives, body(): lax.all_to_all(both.transpose(1, 0, 2, 3), 'ctx', 0, 0, axis_index_groups...  5.07 us
    dot_general x1, matrix products, body(): jnp.dot(compact(part), fc_feature, preferred_element_type=jnp.float32)  4.81 us
    dot_general x1, matrix products, body(): jnp.dot(compact(embed_cols), fc_embed, preferred_element_type=jnp.float32)  4.81 us
    unnamed x8, local copies, waits for them, and re-layouts  3.76 us
  transfers between devices with their start and end apart: 1, of which 0 were waited for; matrix products, arithmetic and copies ran while one was open for 8% of the time, Pallas kernels for 22%

profile of v2, /device:TPU:29, one launch (start us, length us, event | category | flops | bytes accessed | tf_op | source)
XLA Modules:
  0.0 133.8 jit_solution(14873498600388134879)
XLA Ops:
  0.7 0.7 iota_compare_fusion.7
  1.4 1.2 fusion.1
  2.6 0.1 select_reduce_fusion.1
  2.8 0.1 copy.51
  2.9 0.1 and_select_fusion
  3.0 0.1 copy.52.mask_ref
  3.1 0.9 copy_bitcast_fusion
  4.0 1.0 copy.50
  5.0 0.8 fusion.10
  5.7 0.1 broadcast_in_dim.34
  5.8 0.0 copy-start.1
  5.9 1.2 copy-done.1
  7.1 0.0 copy-start.2
  7.1 1.2 copy-done.2
  8.3 70.7 %shard_map.122 = (f32[1024,128]{1,0:T(8,128)S(1)}, f32[1024,128]{1,0:T(8,128)S(1)}, bf16[16,32,128]{2,1,0:T(8,128)(2,1)S(1)}) custom-call(bf16[16,128,128]{2,1,0:T(8,128)(2,1)S(1)} %pad_maximum_fusion.1.small_ref, bf16[512,1024]{1,0:T(8,128)(2,1)S(1)} %copy-done.1, bf16[512,1024]{1,0:T(8,128)(2,1)S(1)} %copy-done.2, f32[128,256]{1,0:T(8,128)S(1)} %copy.52.mask_ref), custom_call_target="tpu_custom_call" | custom-call | flops 2147483648 | bytes 2097152 | tf_op jit(solution)/shard_map/pallas_call | solution.py:328
  79.0 0.1 pad_maximum_fusion
  79.1 0.3 reshape.155
  79.4 0.6 copy.53
  80.0 5.1 %all_to_all.21 = f32[2,128,4,256]{1,2,3,0:T(4,128)S(1)} all-to-all(f32[2,128,4,256]{1,2,3,0:T(4,128)S(1)} %bitcast.65), channel_id=1, replica_groups={{0,1},{2,3},{4,5},{6,7},{8,9},{10,11},{12,13},{14,15},{16,17},{18,19},{..., dimensions={0} | all-to-all | bytes 2097152 | tf_op jit(solution)/shard_map/all_to_all | solution.py:364
  85.1 0.1 fusion.5
  85.2 0.1 copy.56
  85.4 0.1 divide_convert_fusion
  85.5 0.1 copy.57
  85.6 0.7 convert_element_type.60
  86.4 6.0 %all-to-all-start.1 = ((bf16[16,8,512]{2,1,0:T(8,128)(2,1)}), bf16[16,8,512]{2,1,0:T(8,128)(2,1)S(1)}, u32[]{:S(2)}, u32[]{:S(2)}) async-start(bf16[16,8,512]{2,1,0:T(8,128)(2,1)} %convert_element_type.60), calls=%async_computation.1 | async-start | bytes 262144 | tf_op jit(solution)/shard_map/all_to_all | solution.py:374
  92.4 0.1 copy.58
  92.5 0.1 broadcast_in_dim.55
  92.6 0.1 select_reduce_fusion
  92.7 0.1 reshape.156
  92.8 0.0 copy-start
  92.8 4.8 %fusion.4 = f32[16,8192]{1,0:T(8,128)S(1)} fusion(bf16[512,8192]{1,0:T(8,128)(2,1)} %param.17, bf16[128,512]{1,0:T(8,128)(2,1)S(1)} %reshape.156, s32[128]{0:T(128)S(1)} %convert_element_type.62, pred[128]{0:T(512)(128)(4,1)S(1)} %broadcast_compare_fusion), kind=kOutput, calls=%fused_computation.10 | convolution fusion | flops 136327168 | bytes 9044608 | tf_op jit(solution)/shard_map/dot_general | solution.py:379
  97.6 4.8 %convolution_add_fusion.joined_ref = f32[16,8192]{1,0:T(8,128)S(1)} fusion(f32[16,8192]{1,0:T(8,128)S(1)} %fusion.4, bf16[512,8192]{1,0:T(8,128)(2,1)} %param.18, bf16[128,512]{0,1:T(8,128)(2,1)S(1)} %bitcast.67, s32[128]{0:T(128)S(1)} %convert_element_type.62, pred[128]{0:T(512)(128)(4,1)S(1)} %broadcast_compare_fusion), kind=kOutput, calls=%fused_computation | convolution fusion | flops 136460288 | bytes 9568896 | tf_op jit(solution)/shard_map/dot_general | solution.py:380
  102.5 0.1 fusion.15
  102.6 0.0 copy-done
  102.6 29.9 %shard_map.123 = bf16[8,8192]{1,0:T(8,128)(2,1)S(1)} custom-call(f32[16,8192]{1,0:T(8,128)S(1)} %convolution_add_fusion.joined_ref, f32[1,8192]{1,0:T(1,128)S(1)} %bitcast.64, bf16[8,16]{1,0:T(8,128)(2,1)S(1)} %dynamic-slice_bitcast_fusion.pick_ref), custom_call_target="tpu_custom_call" | custom-call | tf_op jit(solution)/shard_map/pallas_call | solution.py:383
  132.5 0.0 all-to-all-done.1
  132.5 0.7 copy.67
  133.2 0.7 copy.68
  (12 shorter events, 0.2 us)
Async XLA Ops:
  5.8 1.2 copy-start.1
  7.1 1.2 copy-start.2
  86.4 46.1 %all-to-all-start.1 = ((bf16[16,8,512]{2,1,0:T(8,128)(2,1)}), bf16[16,8,512]{2,1,0:T(8,128)(2,1)S(1)}, u32[]{:S(2)}, u32[]{:S(2)}) async-start(bf16[16,8,512]{2,1,0:T(8,128)(2,1)} %convert_element_type.60), calls=%async_computation.1 | async-start | bytes 262144 | tf_op jit(solution)/shard_map/all_to_all | solution.py:374
  92.8 9.8 %copy-start = (f32[8192]{0:T(1024)S(1)}, f32[8192]{0:T(1024)}, u32[]{:S(2)}) copy-start(f32[8192]{0:T(1024)} %param.19) | copy-start | bytes 98308

commit v3 on v2

--- a/solution.py
+++ b/solution.py
@@ -198,58 +198,107 @@
 
 
 def join_kernel(
-    n, joined_ref, gain_ref, pick_ref, out_ref, pieces, sums, send_a, recv_a, send_b, recv_b
+    n,
+    pick_ref,
+    joined_ref,
+    gain_ref,
+    part_ref,
+    draft_ref,
+    attended_ref,
+    pieces,
+    rows,
+    attended,
+    send_a,
+    recv_a,
+    send_b,
+    recv_b,
+    send_c,
+    recv_c,
 ):
     me = lax.axis_index("ctx")
-    width = pieces.shape[2]
+    slots = joined_ref.shape[0]
     greet(n, me)
-
-    def columns(d):
-        return joined_ref.at[:, pl.ds(pl.multiple_of(d * width, width), width)]
 
     def piece(r):
         to = lax.rem(me + r, n)
-        return push(columns(to), pieces.at[me], send_a.at[r], recv_a.at[me], to)
-
-    def total(r):
+        return push(joined_ref.at[to], pieces.at[me], send_a.at[r], recv_a.at[me], to)
+
+    def finished(r):
         to = lax.rem(me + r, n)
-        return push(sums.at[me], sums.at[me], send_b.at[r], recv_b.at[me], to)
-
-    @pl.loop(1, n)
-    def _(r):
-        piece(r).start()
-
-    pieces[me] = joined_ref[:, pl.ds(pl.multiple_of(me * width, width), width)]
+        return push(rows.at[me], rows.at[me], send_b.at[r], recv_b.at[me], to)
+
+    def part(r):
+        to = lax.rem(me + r, n)
+        return push(part_ref.at[to], attended.at[me], send_c.at[r], recv_c.at[me], to)
+
+    @pl.loop(1, n)
+    def _(r):
+        @pl.when(lax.rem(me + r, n) < slots)
+        def _():
+            piece(r).start()
+
+    @pl.loop(1, n)
+    def _(r):
+        part(r).start()
+
+    attended[me] = part_ref[me]
+
+    @pl.when(me < slots)
+    def _():
+        pieces[me] = joined_ref[me]
+
+        @pl.loop(1, n)
+        def _(r):
+            source = lax.rem(me - r + n, n)
+            push(
+                pieces.at[source], pieces.at[source], send_a.at[r], recv_a.at[source], source
+            ).wait_recv()
+
+        joined = jnp.sum(pieces[...], axis=0)
+        squares = jnp.sum(jnp.sum(joined * joined, axis=0, keepdims=True), axis=1, keepdims=True)
+        inverse = lax.rsqrt(squares / joined.size + 1e-06)
+        rows[me] = (joined * inverse * gain_ref[...]).astype(jnp.bfloat16)
+
+        @pl.loop(1, n)
+        def _(r):
+            finished(r).start()
 
     @pl.loop(1, n)
     def _(r):
         source = lax.rem(me - r + n, n)
-        push(pieces.at[source], pieces.at[source], send_a.at[r], recv_a.at[source], source).wait_recv()
-
-    sums[me] = jnp.sum(pieces[...], axis=0)
-
-    @pl.loop(1, n)
-    def _(r):
-        total(r).start()
+        push(
+            attended.at[source], attended.at[source], send_c.at[r], recv_c.at[source], source
+        ).wait_recv()
+
+    attended_ref[...] = attended[...]
 
     @pl.loop(1, n)
     def _(r):
         source = lax.rem(me - r + n, n)
-        push(sums.at[source], sums.at[source], send_b.at[r], recv_b.at[source], source).wait_recv()
-
-    joined = sums[...]
-    squares = jnp.sum(jnp.sum(joined * joined, axis=0), axis=1, keepdims=True)
-    inverse = lax.rsqrt(squares / (n * width) + 1e-06)
-    for d in range(n):
-        normed = sums[d] * inverse * gain_ref[:, d * width : (d + 1) * width]
-        out_ref[:, d * width : (d + 1) * width] = jnp.dot(
-            pick_ref[...], normed.astype(jnp.bfloat16), preferred_element_type=jnp.float32
-        ).astype(jnp.bfloat16)
-
-    @pl.loop(1, n)
-    def _(r):
-        piece(r).wait_send()
-        total(r).wait_send()
+
+        @pl.when(source < slots)
+        def _():
+            push(
+                rows.at[source], rows.at[source], send_b.at[r], recv_b.at[source], source
+            ).wait_recv()
+
+    for row in range(draft_ref.shape[0]):
+        total = jnp.zeros(draft_ref.shape[1:], jnp.float32)
+        for slot in range(slots):
+            total = total + pick_ref[row, slot] * rows[slot].astype(jnp.float32)
+        draft_ref[row] = total.astype(jnp.bfloat16)
+
+    @pl.loop(1, n)
+    def _(r):
+        @pl.when(lax.rem(me + r, n) < slots)
+        def _():
+            piece(r).wait_send()
+
+        part(r).wait_send()
+
+        @pl.when(me < slots)
+        def _():
+            finished(r).wait_send()
 
 
 def body(
@@ -371,32 +420,39 @@
     num = jnp.sum(num * factor[..., None], axis=0)
     den = jnp.sum(den * factor, axis=0)
     part = (num / den[..., None]).reshape(every_row, own_cols).astype(jnp.bfloat16)
-    attended = lax.all_to_all(part, "ctx", 0, 1, tiled=True)
+    parts = jnp.pad(
+        part.reshape(n, owned * part_heads, HEAD_WIDTH),
+        ((0, 0), (0, embed_rows - owned * part_heads), (0, 0)),
+    )
 
     def compact(x):
         return jnp.dot(pick, x, preferred_element_type=jnp.float32).astype(jnp.bfloat16)
 
     joined = jnp.dot(compact(embed_cols), fc_embed, preferred_element_type=jnp.float32)
     joined = joined + jnp.dot(compact(part), fc_feature, preferred_element_type=jnp.float32)
-    own_pick = lax.dynamic_slice_in_dim(pick, me * owned, owned, 1).T
-    width = joined.shape[1] // n
-    draft_input = pl.pallas_call(
+    own_pick = lax.dynamic_slice_in_dim(pick, me * owned, owned, 1).T.astype(jnp.float32)
+    lanes = (joined.shape[1] // HEAD_WIDTH, HEAD_WIDTH)
+    draft, arrived = pl.pallas_call(
         functools.partial(join_kernel, n),
-        out_shape=jax.ShapeDtypeStruct(token_embed.shape, jnp.bfloat16),
-        in_specs=[in_vmem] * 3,
-        out_specs=in_vmem,
+        out_shape=[
+            jax.ShapeDtypeStruct((owned,) + lanes, jnp.bfloat16),
+            jax.ShapeDtypeStruct(parts.shape, jnp.bfloat16),
+        ],
+        in_specs=[pl.BlockSpec(memory_space=pltpu.SMEM)] + [in_vmem] * 3,
+        out_specs=[in_vmem] * 2,
         scratch_shapes=[
-            pltpu.VMEM((n, slots, width), jnp.float32),
-            pltpu.VMEM((n, slots, width), jnp.float32),
-            pltpu.SemaphoreType.DMA((n,)),
-            pltpu.SemaphoreType.DMA((n,)),
-            pltpu.SemaphoreType.DMA((n,)),
-            pltpu.SemaphoreType.DMA((n,)),
-        ],
+            pltpu.VMEM((n,) + lanes, jnp.float32),
+            pltpu.VMEM((slots,) + lanes, jnp.bfloat16),
+            pltpu.VMEM(parts.shape, jnp.bfloat16),
+        ]
+        + [pltpu.SemaphoreType.DMA((n,))] * 6,
         compiler_params=pltpu.CompilerParams(
             collective_id=1, has_side_effects=True, vmem_limit_bytes=24 * 1024 * 1024
         ),
-    )(joined, draft_gain[None, :], own_pick)
+    )(own_pick, joined.reshape((slots,) + lanes), draft_gain.reshape(lanes), parts)
+    draft_input = draft.reshape(owned, -1)
+    attended = arrived[:, : owned * part_heads].reshape(n, owned, own_cols)
+    attended = attended.transpose(1, 0, 2).reshape(owned, -1)
     return (attended, draft_input)
 
 

time: 134 us -> 127 us (0.948)
  the two profiles are of different devices: /device:TPU:29 before, /device:TPU:0 now
where the time goes in v3:
time: 127 us
  Pallas kernels  101 us (80%)
  matrix products  11 us (9%)
  local copies, waits for them, and re-layouts  7.59 us (6%)
  blocking collectives  4.58 us (4%)
  other arithmetic  2.3 us (2%)
    pallas_call x1, Pallas kernels, body(): pl.pallas_call(functools.partial(attention_kernel, n, q_rows, tree_rows),...  60.1 us
    pallas_call x1, Pallas kernels, body(): pl.pallas_call(functools.partial(join_kernel, n), out_shape=[jax.ShapeDty...  40.7 us
    dot_general x1, matrix products, body(): jnp.dot(compact(part), fc_feature, preferred_element_type=jnp.float32)  4.81 us
    dot_general x1, matrix products, body(): jnp.dot(compact(embed_cols), fc_embed, preferred_element_type=jnp.float32)  4.81 us
    all_to_all x1, blocking collectives, body(): lax.all_to_all(both.transpose(1, 0, 2, 3), 'ctx', 0, 0, axis_index_groups...  4.58 us
    unnamed x8, local copies, waits for them, and re-layouts  3.3 us

profile of v3, /device:TPU:0, one launch (start us, length us, event | category | flops | bytes accessed | tf_op | source)
XLA Modules:
  0.0 127.1 jit_solution(17474751216677326675)
XLA Ops:
  0.7 0.7 iota_compare_fusion.7
  1.4 1.2 fusion.2
  2.6 0.1 select_reduce_fusion.1
  2.8 0.1 copy.45
  2.9 0.1 and_select_fusion
  3.0 0.1 copy.46.mask_ref
  3.1 0.9 copy_bitcast_fusion.1
  4.0 1.0 copy.44
  5.0 0.8 fusion.12
  5.7 0.1 broadcast_in_dim.53
  5.8 0.0 copy-start.1
  5.9 1.2 copy-done.1
  7.1 0.0 copy-start.2
  7.1 1.2 copy-done.2
  8.3 60.1 %shard_map.122 = (f32[1024,128]{1,0:T(8,128)S(1)}, f32[1024,128]{1,0:T(8,128)S(1)}, bf16[16,32,128]{2,1,0:T(8,128)(2,1)S(1)}) custom-call(bf16[16,128,128]{2,1,0:T(8,128)(2,1)S(1)} %pad_maximum_fusion.1.small_ref, bf16[512,1024]{1,0:T(8,128)(2,1)S(1)} %copy-done.1, bf16[512,1024]{1,0:T(8,128)(2,1)S(1)} %copy-done.2, f32[128,256]{1,0:T(8,128)S(1)} %copy.46.mask_ref), custom_call_target="tpu_custom_call" | custom-call | flops 2147483648 | bytes 2097152 | tf_op jit(solution)/shard_map/pallas_call | solution.py:377
  68.4 0.1 pad_maximum_fusion
  68.5 0.3 reshape.168
  68.8 0.6 copy.47
  69.4 4.6 %all_to_all.5 = f32[2,128,4,256]{1,2,3,0:T(4,128)S(1)} all-to-all(f32[2,128,4,256]{1,2,3,0:T(4,128)S(1)} %bitcast.79), channel_id=1, replica_groups={{0,1},{2,3},{4,5},{6,7},{8,9},{10,11},{12,13},{14,15},{16,17},{18,19},{..., dimensions={0} | all-to-all | bytes 2097152 | tf_op jit(solution)/shard_map/all_to_all | solution.py:413
  74.0 0.1 fusion.6
  74.1 0.2 copy.51
  74.3 0.1 copy.52
  74.4 0.1 divide_convert_fusion
  74.5 0.1 broadcast_in_dim.50
  74.6 0.1 select_reduce_fusion
  74.7 0.1 div.35
  74.8 0.1 reshape.167
  74.9 0.1 fusion.19
  75.0 0.0 copy-start
  75.0 4.8 %fusion.5 = f32[16,8192]{1,0:T(8,128)S(1)} fusion(bf16[512,8192]{1,0:T(8,128)(2,1)} %param.17, bf16[128,512]{1,0:T(8,128)(2,1)S(1)} %reshape.167, s32[128]{0:T(128)S(1)} %convert_element_type.62, pred[128]{0:T(512)(128)(4,1)S(1)} %broadcast_compare_fusion), kind=kOutput, calls=%fused_computation.11 | convolution fusion | flops 136327168 | bytes 9044608 | tf_op jit(solution)/shard_map/dot_general | solution.py:431
  79.8 4.8 %fusion = f32[2,8,64,128]{3,1,2,0:T(8,128)S(1)} fusion(f32[16,8192]{1,0:T(8,128)S(1)} %fusion.5, bf16[512,8192]{1,0:T(8,128)(2,1)} %param.18, bf16[128,512]{0,1:T(8,128)(2,1)S(1)} %bitcast.82, s32[128]{0:T(128)S(1)} %convert_element_type.62, pred[128]{0:T(512)(128)(4,1)S(1)} %broadcast_compare_fusion), kind=kOutput, calls=%fused_computation.1 | convolution fusion | flops 136460288 | bytes 9568896 | tf_op jit(solution)/shard_map/dot_general | solution.py:432
  84.6 0.1 copy.56
  84.7 0.1 fusion.10.part_ref
  84.9 0.0 copy-done
  84.9 40.7 %shard_map.123 = (bf16[8,64,128]{2,1,0:T(8,128)(2,1)S(1)}, bf16[16,32,128]{2,1,0:T(8,128)(2,1)S(1)}) custom-call(f32[8,16]{1,0:T(8,128)S(1)} %convert_bitcast_fusion.pick_ref, f32[16,64,128]{2,1,0:T(8,128)S(1)} %bitcast.76, f32[64,128]{1,0:T(8,128)S(1)} %bitcast.78, bf16[16,32,128]{2,1,0:T(8,128)(2,1)S(1)} %fusion.10.part_ref), custom_call_target="tpu_custom_call" | custom-call | tf_op jit(solution)/shard_map/pallas_call | solution.py:435
  125.6 0.7 reshape.171
  126.3 0.7 copy.62
  (13 shorter events, 0.2 us)
Async XLA Ops:
  5.8 1.2 copy-start.1
  7.1 1.2 copy-start.2
  75.0 9.9 %copy-start = (f32[8192]{0:T(1024)S(1)}, f32[8192]{0:T(1024)}, u32[]{:S(2)}) copy-start(f32[8192]{0:T(1024)} %param.19) | copy-start | bytes 98308

commit v4 on v3

--- a/solution.py
+++ b/solution.py
@@ -61,10 +61,13 @@
     k_ref,
     v_ref,
     mask_ref,
+    expand_ref,
+    fc_ref,
     num_ref,
     stat_ref,
-    embed_ref,
+    joined_ref,
     small,
+    fc,
     keys,
     values,
     tree_k,
@@ -82,6 +85,7 @@
     me = lax.axis_index("ctx")
     mine = me // members
     member = lax.rem(me, members)
+    weights = pltpu.make_async_copy(fc_ref, fc, local_sem.at[3])
     greet(n, me)
 
     def small_copy(r):
@@ -118,6 +122,7 @@
     ]
     for copy in own:
         copy.start()
+    weights.start()
     for copy in own:
         copy.wait()
 
@@ -158,7 +163,6 @@
 
     tree_k[...] = small[:, q_rows : q_rows + tree_rows, :].reshape(tree_k.shape)
     tree_v[...] = small[:, q_rows + tree_rows : q_rows + 2 * tree_rows, :].reshape(tree_v.shape)
-    embed_ref[...] = small[:, q_rows + 2 * tree_rows :, :]
     tiles = n // stack
 
     @pl.loop(0, tiles)
@@ -167,6 +171,20 @@
         mask = mask_ref[pl.ds(start, rows_of_tile), :]
         mask = jnp.broadcast_to(mask[:, None, :], (rows_of_tile, GROUP, mask.shape[1]))
         step(t, tree_k[...], tree_v[...], mask.reshape(tile, mask.shape[2]), True)
+
+    embed = small[:, q_rows + 2 * tree_rows :, :].reshape(expand_ref.shape[2], HEAD_WIDTH)
+    kept = [
+        jnp.dot(expand_ref[h], embed, preferred_element_type=jnp.float32).astype(jnp.bfloat16)
+        for h in range(expand_ref.shape[0])
+    ]
+    kept = jnp.concatenate(kept, axis=1)
+    weights.wait()
+    chunk = 8 * HEAD_WIDTH
+
+    @pl.loop(0, fc.shape[1] // chunk)
+    def _(c):
+        cols = pl.ds(pl.multiple_of(c * chunk, chunk), chunk)
+        joined_ref[:, cols] = jnp.dot(kept, fc[:, cols], preferred_element_type=jnp.float32)
 
     @pl.loop(0, KEY_HEADS)
     def _(r):
@@ -374,17 +392,25 @@
     ).reshape(every_row, n * tree_rows)
     any_space = pl.BlockSpec(memory_space=pl.ANY)
     in_vmem = pl.BlockSpec(memory_space=pltpu.VMEM)
-    num, stat, embed = pl.pallas_call(
+    expand = pick.reshape(slots, n, owned, 1)[None] * jnp.eye(
+        part_heads, dtype=jnp.bfloat16
+    ).reshape(part_heads, 1, 1, 1, part_heads)
+    expand = jnp.pad(
+        expand.reshape(part_heads, slots, n, owned * part_heads),
+        ((0, 0), (0, 0), (0, 0), (0, embed_rows - owned * part_heads)),
+    ).reshape(part_heads, slots, n * embed_rows)
+    num, stat, joined = pl.pallas_call(
         functools.partial(attention_kernel, n, q_rows, tree_rows),
         out_shape=[
             jax.ShapeDtypeStruct((every_row * GROUP, HEAD_WIDTH), jnp.float32),
             jax.ShapeDtypeStruct((every_row * GROUP, HEAD_WIDTH), jnp.float32),
-            jax.ShapeDtypeStruct((n, embed_rows, HEAD_WIDTH), jnp.bfloat16),
+            jax.ShapeDtypeStruct((slots, fc_embed.shape[1]), jnp.float32),
         ],
-        in_specs=[any_space] * 3 + [in_vmem],
+        in_specs=[any_space] * 3 + [in_vmem] * 2 + [any_space],
         out_specs=[in_vmem] * 3,
         scratch_shapes=[
             pltpu.VMEM(small.shape, jnp.bfloat16),
+            pltpu.VMEM(fc_embed.shape, jnp.bfloat16),
             pltpu.VMEM((KEY_HEADS, positions, HEAD_WIDTH), jnp.bfloat16),
             pltpu.VMEM((KEY_HEADS, positions, HEAD_WIDTH), jnp.bfloat16),
             pltpu.VMEM((n * tree_rows, HEAD_WIDTH), jnp.bfloat16),
@@ -395,7 +421,7 @@
             pltpu.SemaphoreType.DMA((n,)),
             pltpu.SemaphoreType.DMA((2, KEY_HEADS)),
             pltpu.SemaphoreType.DMA((2, KEY_HEADS)),
-            pltpu.SemaphoreType.DMA((3,)),
+            pltpu.SemaphoreType.DMA((4,)),
         ],
         compiler_params=pltpu.CompilerParams(
             collective_id=0, has_side_effects=True, vmem_limit_bytes=40 * 1024 * 1024
@@ -405,8 +431,7 @@
             bytes_accessed=4 * prefix_key_heads.size,
             transcendentals=every_row * GROUP * positions * KEY_HEADS,
         ),
-    )(small, prefix_key_heads, prefix_value_heads, allowed)
-    embed_cols = embed[:, : owned * part_heads].reshape(every_row, own_cols)
+    )(small, prefix_key_heads, prefix_value_heads, allowed, expand, fc_embed)
     both = jnp.concatenate([num, stat], axis=1).reshape(
         every_row, members, part_heads, 2 * HEAD_WIDTH
     )
@@ -428,7 +453,6 @@
     def compact(x):
         return jnp.dot(pick, x, preferred_element_type=jnp.float32).astype(jnp.bfloat16)
 
-    joined = jnp.dot(compact(embed_cols), fc_embed, preferred_element_type=jnp.float32)
     joined = joined + jnp.dot(compact(part), fc_feature, preferred_element_type=jnp.float32)
     own_pick = lax.dynamic_slice_in_dim(pick, me * owned, owned, 1).T.astype(jnp.float32)
     lanes = (joined.shape[1] // HEAD_WIDTH, HEAD_WIDTH)

time: 127 us -> 127 us (level)
  matrix products: 11 us -> 6.15 us
  local copies, waits for them, and re-layouts: 7.59 us -> 11.4 us
    dot_general x1 -> x0, matrix products: 4.81 us -> none  [body(): jnp.dot(compact(embed_cols), fc_embed, preferred_element_type=jnp.float32)]
    unnamed x8 -> x10, local copies, waits for them, and re-layouts: 3.3 us -> 6.68 us
where the time goes in v4:
time: 127 us; the launch traced here: 126 us
  Pallas kernels  101 us (80%)
  local copies, waits for them, and re-layouts  11.4 us (9%)
  matrix products  6.15 us (5%)
  blocking collectives  4.58 us (4%)
  other arithmetic  2.44 us (2%)
    pallas_call x1, Pallas kernels, body(): pl.pallas_call(functools.partial(attention_kernel, n, q_rows, tree_rows),...  60.1 us
    pallas_call x1, Pallas kernels, body(): pl.pallas_call(functools.partial(join_kernel, n), out_shape=[jax.ShapeDty...  40.7 us
    unnamed x10, local copies, waits for them, and re-layouts  6.68 us
    dot_general x1, matrix products, body(): jnp.dot(compact(part), fc_feature, preferred_element_type=jnp.float32)  4.81 us
    all_to_all x1, blocking collectives, body(): lax.all_to_all(both.transpose(1, 0, 2, 3), 'ctx', 0, 0, axis_index_groups...  4.58 us

profile of v4, /device:TPU:0, one launch (start us, length us, event | category | flops | bytes accessed | tf_op | source)
XLA Modules:
  0.0 126.2 jit_solution(16331955565655477656)
XLA Ops:
  0.7 0.7 iota_compare_fusion.9
  1.4 1.2 fusion.2
  2.6 0.1 select_reduce_fusion.1
  2.8 0.1 broadcast_in_dim.50
  2.9 0.1 copy.49
  3.0 0.1 and_select_fusion
  3.1 0.1 copy.51.mask_ref
  3.2 0.1 select_reduce_fusion
  3.3 0.1 convert_element_type.82
  3.4 0.1 gt.23
  3.5 0.1 fusion.18
  3.6 0.1 copy.50
  3.7 0.2 mul.43
  3.9 0.9 copy_bitcast_fusion.1
  4.9 1.0 copy.48
  5.8 0.8 fusion.11
  6.6 0.1 broadcast_in_dim.53
  6.7 0.0 copy-start
  6.7 3.4 %copy-done = bf16[512,8192]{1,0:T(8,128)(2,1)S(1)} copy-done((bf16[512,8192]{1,0:T(8,128)(2,1)S(1)}, bf16[512,8192]{1,0:T(8,128)(2,1)}, u32[]{:S(2)}) %copy-start) | copy-done | bytes 8388632
  10.1 0.0 copy-start.1
  10.1 1.2 copy-done.1
  11.3 0.0 copy-start.2
  11.3 1.2 copy-done.2
  12.5 60.1 %shard_map.122 = (f32[1024,128]{1,0:T(8,128)S(1)}, f32[1024,128]{1,0:T(8,128)S(1)}, f32[16,8192]{1,0:T(8,128)S(1)}) custom-call(bf16[16,128,128]{2,1,0:T(8,128)(2,1)S(1)} %pad_maximum_fusion.1.small_ref, bf16[512,1024]{1,0:T(8,128)(2,1)S(1)} %copy-done.1, bf16[512,1024]{1,0:T(8,128)(2,1)S(1)} %copy-done.2, f32[128,256]{1,0:T(8,128)S(1)} %copy.51.mask_ref, ...), custom_call_target="tpu_custom_call" | custom-call | flops 2147483648 | bytes 2097152 | tf_op jit(solution)/shard_map/pallas_call | solution.py:402
  72.7 0.1 pad_maximum_fusion
  72.7 0.3 reshape.207
  73.0 0.0 copy-start.3
  73.1 0.6 copy.52
  73.6 4.6 %all_to_all.5 = f32[2,128,4,256]{1,2,3,0:T(4,128)S(1)} all-to-all(f32[2,128,4,256]{1,2,3,0:T(4,128)S(1)} %bitcast.80), channel_id=1, replica_groups={{0,1},{2,3},{4,5},{6,7},{8,9},{10,11},{12,13},{14,15},{16,17},{18,19},{..., dimensions={0} | all-to-all | bytes 2097152 | tf_op jit(solution)/shard_map/all_to_all | solution.py:438
  78.2 0.1 fusion.5
  78.4 0.2 copy.56
  78.6 0.1 copy.57
  78.7 0.1 divide_convert_fusion
  78.8 0.1 div.35
  78.9 0.1 fusion.16
  79.0 4.8 %fusion = f32[2,8,64,128]{3,1,2,0:T(8,128)S(1)} fusion(f32[16,8192]{1,0:T(8,128)S(1)} %get-tuple-element.7, bf16[512,8192]{1,0:T(8,128)(2,1)} %param.18, bf16[128,512]{0,1:T(8,128)(2,1)S(1)} %bitcast.83, s32[128]{0:T(128)S(1)} %convert_element_type.76, pred[128]{0:T(512)(128)(4,1)S(1)} %broadcast_compare_fusion.1), kind=kOutput, calls=%fused_computation.1 | convolution fusion | flops 136460288 | bytes 9568896 | tf_op jit(solution)/shard_map/dot_general | solution.py:456
  83.8 0.1 copy.61
  83.9 0.1 fusion.9.part_ref
  84.1 0.0 copy-done.3
  84.1 40.7 %shard_map.123 = (bf16[8,64,128]{2,1,0:T(8,128)(2,1)S(1)}, bf16[16,32,128]{2,1,0:T(8,128)(2,1)S(1)}) custom-call(f32[8,16]{1,0:T(8,128)S(1)} %convert_bitcast_fusion.pick_ref, f32[16,64,128]{2,1,0:T(8,128)S(1)} %bitcast.77, f32[64,128]{1,0:T(8,128)S(1)} %bitcast.79, bf16[16,32,128]{2,1,0:T(8,128)(2,1)S(1)} %fusion.9.part_ref), custom_call_target="tpu_custom_call" | custom-call | tf_op jit(solution)/shard_map/pallas_call | solution.py:459
  124.7 0.7 reshape.210
  125.5 0.7 copy.67
  (18 shorter events, 0.3 us)
Async XLA Ops:
  6.7 3.4 %copy-start = (bf16[512,8192]{1,0:T(8,128)(2,1)S(1)}, bf16[512,8192]{1,0:T(8,128)(2,1)}, u32[]{:S(2)}) copy-start(bf16[512,8192]{1,0:T(8,128)(2,1)} %fc_ref.1) | copy-start | bytes 25165828
  10.1 1.2 copy-start.1
  11.3 1.2 copy-start.2
  73.0 11.0 %copy-start.3 = (f32[8192]{0:T(1024)S(1)}, f32[8192]{0:T(1024)}, u32[]{:S(2)}) copy-start(f32[8192]{0:T(1024)} %param.19) | copy-start | bytes 98308
